TPU v7x, 32 devices: a whole 2x2x4 slice. The times are simulated.
32 devices in a mesh: grp: 2 (over x), tile: 8 (over z, y), tok: 2 (over core).
Axes of the slice: x: 2, y: 2, z: 4, core: 2. Of those that a mesh axis runs over, the one named last changes fastest.
Arguments:
- resid: bfloat16 [3584, 8192], P(('grp', 'tok'), 'tile'), parts along dimension 0, may hold values from -17 to 17, as said below
- labels: int32 [3584], P('grp'), parts along dimension 0, may hold values from 0 to 2047
- owner: int32 [216], replicated, may hold values from 0 to 215, each once
Outputs:
- cov_tiles: float32 [432, 512, 512], P(('grp', 'tile'), 'tok'), parts along dimension 0
There are 2 independent parts, one for each index of `grp`. A program takes and returns all parts, laid end to end along the dimension named above; an argument that names none is the same for every part. Nothing has to cross between parts.
Inputs may be any that keep to these rules, and one draw needn't show every extreme that they name: resid has per-column offsets and scales. owner is a permutation; owner[t] for t < 210 is the slot of task t, and the other entries name empty slots.
All inputs are finite; a program needn't handle non-finite values.
Results may differ from a plain program's by a relative error of at most 0.0003.
Values may be sent and summed in bfloat16 or wider, within the bound.
A program may use at most 192 MiB of HBM per device.

v0:
```python
import jax
import jax.numpy as jnp
import numpy as np
from jax import lax
from jax.sharding import PartitionSpec as P

C = 2048
TILE = 512
PANELS = 20
TASKS = 210


def pair_table(count):
    firsts, seconds = np.triu_indices(count)
    return np.stack([firsts, seconds], 1).astype(np.int32)


def label_panel(marks):
    return (marks[:, None] == jnp.arange(C, dtype=jnp.int32)[None, :]).astype(jnp.bfloat16)


def dense_rows(matrix, first, second, start, count):
    left = lax.dynamic_slice_in_dim(matrix, first * TILE + start, count, 1)
    right = lax.dynamic_slice_in_dim(matrix, second * TILE, TILE, 1)
    return lax.dot_general(
        left, right, (((0,), (0,)), ((), ())), preferred_element_type=jnp.float32
    )


def task_pairs():
    return jnp.asarray(np.concatenate([pair_table(PANELS), np.zeros((1, 2), np.int32)], 0))


def owned_tiles(matrix, tasks, start, count):
    pairs = task_pairs()

    def owned_one(task):
        pick = jnp.minimum(task, TASKS)
        first = pairs[pick, 0]
        second = pairs[pick, 1]
        block = dense_rows(matrix, first, second, start, count)
        return jnp.where(task < TASKS, block, 0.0)

    return lax.map(owned_one, tasks)


def centre_tiles(raw, tasks, means, start, count, total_rows):
    pairs = task_pairs()

    def centre_one(block, task):
        pick = jnp.minimum(task, TASKS)
        left_mean = lax.dynamic_slice_in_dim(means, pairs[pick, 0] * TILE + start, count)
        right_mean = lax.dynamic_slice_in_dim(means, pairs[pick, 1] * TILE, TILE)
        value = block / total_rows - left_mean[:, None] * right_mean[None, :]
        return jnp.where(task < TASKS, value, 0.0)

    return jax.vmap(centre_one)(raw, tasks)


def body(resid, labels, owner):
    tiles_count = lax.axis_size("tile")
    own = owner.shape[0] // tiles_count
    place = lax.axis_index("tile")
    half = lax.axis_index("tok")
    inverse = (
        jnp.full(owner.shape, TASKS, jnp.int32)
        .at[owner[:TASKS]]
        .set(jnp.arange(TASKS, dtype=jnp.int32))
    )
    tasks = lax.dynamic_slice_in_dim(inverse, place * own, own)
    total_rows = labels.shape[0]
    count = TILE // lax.axis_size("tok")
    start = half * count
    columns = lax.all_gather(resid, "tile", axis=1, tiled=True)
    rows_here = columns.shape[0]
    marks = lax.dynamic_slice_in_dim(labels, half * rows_here, rows_here)
    matrix = jnp.concatenate([columns, label_panel(marks)], 1)
    partial_sums = jnp.sum(matrix, 0, dtype=jnp.float32)
    means = lax.psum(partial_sums, "tok") / total_rows
    whole = owned_tiles(matrix, tasks, 0, TILE)
    raw = lax.psum_scatter(whole, "tok", scatter_dimension=1, tiled=True)
    return centre_tiles(raw, tasks, means, start, count, total_rows)


def solution(mesh):
    return jax.shard_map(
        body,
        mesh=mesh,
        in_specs=(P(("grp", "tok"), "tile"), P("grp"), P()),
        out_specs=P(("grp", "tile"), "tok", None),
        check_vma=False,
    )
```

profile of v0, /device:TPU:0, one launch (start us, length us, event | category | flops | bytes accessed | tf_op | source)
XLA Modules:
  0.0 533.2 jit_solution(189173653935152614)
XLA Ops:
  12.6 201.7 %all-gather.2.cloned.1.call-done = bf16[896,8192]{1,0:T(8,128)(2,1)} async-done(((bf16[896,1024]{1,0:T(8,128)(2,1)}), bf16[896,8192]{1,0:T(8,128)(2,1)}) %all-gather.2.cloned.1.call-update) | async-done | bytes 14680080 | tf_op jit(solution)/shard_map/all_gather | solution.py:74
  214.3 18.9 %pad_maximum_fusion = bf16[896,10240]{1,0:T(8,128)(2,1)} fusion(bf16[896,2048]{1,0:T(8,128)(2,1)} %fusion.5, bf16[896,8192]{1,0:T(8,128)(2,1)} %all-gather.2.cloned.1.call-done), kind=kLoop, calls=%fused_computation.14 | loop fusion | flops 36700160 | bytes 36700160 | tf_op jit(solution)/shard_map/concatenate | solution.py:77
  233.2 192.2 %while.15 = (s32[]{:T(128)}, f32[27,512,512]{2,1,0:T(8,128)}, s32[27]{0:T(128)S(1)}, bf16[896,10240]{1,0:T(8,128)(2,1)}, s32[]{:T(128)}, /*index=5*/s32[211,2]{1...) while((s32[]{:T(128)}, f32[27,512,512]{2,1,0:T(8,128)}, ...), condition=%wide.region_2.0_spmd.clone, body=%wide.region_1.0_spmd.sunk.clone.sunk | while | flops 470024192 | bytes 2884904 | solution.py:44
  244.2 3.2 fusion.16
  251.4 3.2 fusion.16
  272.7 3.2 fusion.16
  279.8 3.2 fusion.16
  286.9 3.2 fusion.16
  294.0 3.3 fusion.16
  322.5 3.2 fusion.16
  329.7 3.2 fusion.16
  336.8 3.2 fusion.16
  343.9 3.2 fusion.16
  358.1 3.2 fusion.16
  365.2 3.2 fusion.16
  386.6 3.2 fusion.16
  393.7 3.2 fusion.16
  400.8 3.2 fusion.16
  407.9 3.3 fusion.16
  427.0 11.4 %convert_reduce_fusion = f32[10240]{0:T(1024)S(1)} fusion(bf16[896,2048]{1,0:T(8,128)(2,1)} %fusion.5, bf16[896,8192]{1,0:T(8,128)(2,1)} %all-gather.2.cloned.1.call-done), kind=kLoop, calls=%fused_computation.13 | loop fusion | flops 45864960 | bytes 18391040 | tf_op jit(solution)/shard_map/reduce_sum | solution.py:78
  438.4 3.5 psum.7
  441.9 36.5 %while.13 = (s32[]{:T(128)}, f32[10240]{0:T(1024)S(1)}, s32[27,1]{0,1:T(1,128)S(1)}, f32[27,256]{1,0:T(8,128)S(1)}, s32[]{:T(128)}, /*index=5*/s32[]{:T(128)}) while((s32[]{:T(128)}, f32[10240]{0:T(1024)S(1)}, s32[27,1]{0,1:T(1,128)S(1)}, f32[27,256]{1,0:T(8,128)S(1)}, s32[]{:T(128)}, /*index=5*/s32[]{:T(128)}) %tuple.55), condition=%wide.while_cond, body=%wide.while_body.sunk | while | flops 2 | bytes 4185 | solution.py:52
  478.4 36.8 %while.14 = (s32[]{:T(128)}, f32[10240]{0:T(1024)S(1)}, s32[27,1]{0,1:T(1,128)S(1)}, f32[27,512]{1,0:T(8,128)S(1)}, s32[]{:T(128)}, /*index=5*/s32[]{:T(128)}) while((s32[]{:T(128)}, f32[10240]{0:T(1024)S(1)}, s32[27,1]{0,1:T(1,128)S(1)}, f32[27,512]{1,0:T(8,128)S(1)}, s32[]{:T(128)}, /*index=5*/s32[]{:T(128)}) %tuple.63), condition=%wide.while_cond.1, body=%wide.while_body.1.sunk | while | flops 2 | bytes 8281 | solution.py:53
  515.2 11.1 %subtract_select_fusion = f32[27,256,512]{2,1,0:T(8,128)} fusion(f32[27,256,512]{2,1,0:T(8,128)} %reduce-scatter.2.cloned.1.call-done, f32[27,512]{1,0:T(8,128)S(1)} %get-tuple-element.48, f32[27,256]{1,0:T(8,128)S(1)} %get-tuple-element.40, pred[27]{0:T(512)(128)(4,1)S(1)} %get-tuple-element.88), kind=kLoop, calls=%fused_computation.15 | loop fusion | flops 14155776 | bytes 28394524 | tf_op jit(solution)/shard_map/vmap(jit(_where))/select_n | solution.py:55
  (249 shorter events, 150.1 us)
Async XLA Ops:
  6.5 207.8 %all-gather.2.cloned.1.call-start = ((), (), s32[]{:S(2)}) async-start(), calls=%async_computation.1 | async-start | bytes 16515072 | tf_op jit(solution)/shard_map/all_gather | solution.py:74
  7.3 508.0 %reduce-scatter.2.cloned.1.call-start = ((), (), s32[]{:S(2)}) async-start(), calls=%async_computation.2 | async-start | bytes 42467328 | tf_op jit(solution)/shard_map/reduce_scatter | solution.py:81
  12.6 220.6 %copy-start = (s32[211,2]{1,0:T(8,128)S(1)}, s32[211,2]{1,0:T(8,128)}, u32[]{:S(2)}) copy-start(s32[211,2]{1,0:T(8,128)} %constant.67.clone) | copy-start | bytes 5068
Sparse Core Ops, SparseCore 0:
  9.5 204.7 all-gather.1
  425.5 37.7 reduce-scatter.1
where the time goes:
time: 536 us; the launch traced here: 533 us
  waiting for transfers between devices  202 us (38%)
  local copies, waits for them, and re-layouts  111 us (21%)
  matrix products  86.4 us (16%)
  loops' own time  71.6 us (13%)
  other arithmetic  44.7 us (8%)
  between operations  13.5 us (3%)
    all_gather x1, waiting for transfers between devices, body(): columns = lax.all_gather(resid, 'tile', axis=1, tiled=True)  202 us
    dot_general x27, matrix products, dense_rows(): lax.dot_general(left, right, (((0,), (0,)), ((), ())), preferred_element_...  86.4 us
    gather x162, local copies, waits for them, and re-layouts  72.3 us
    another operation x1, loops' own time, owned_tiles(): return lax.map(owned_one, tasks)  70.6 us
    concatenate x1, other arithmetic, body(): matrix = jnp.concatenate([columns, label_panel(marks)], 1)  18.9 us
    dynamic_slice x27, local copies, waits for them, and re-layouts, owned_one(): first = pairs[pick, 0]  17.6 us
    dynamic_slice x27, local copies, waits for them, and re-layouts, owned_tiles(): return lax.map(owned_one, tasks)  17.6 us
    reduce_sum x1, other arithmetic, body(): partial_sums = jnp.sum(matrix, 0, dtype=jnp.float32)  11.4 us
  transfers between devices with their start and end apart: 2, of which 1 were waited for; matrix products, arithmetic and copies ran while one was open for 17% of the time, Pallas kernels for 0%

commit v1 on v0

v1 whole, which is shorter than its diff:
```python
import functools

import jax
import jax.numpy as jnp
import numpy as np
from jax import lax
from jax.experimental import pallas as pl
from jax.experimental.pallas import tpu as pltpu
from jax.sharding import PartitionSpec as P

C = 2048
TILE = 512
PANELS = 20
TASKS = 210
BLK = 256
CHUNK = 128
MESH = pl.DeviceIdType.MESH


def pair_table(count):
    firsts, seconds = np.triu_indices(count)
    return np.stack([firsts, seconds], 1).astype(np.int32)


def kernel(cfg, idx_ref, lab_ref, x_ref, out_ref, *scratch):
    n, Z, Y, npd, own, total_rows = cfg
    g = scratch[:n]
    acc, sums, lsem, osem, rsem, ssem, xs, xr = scratch[n:]
    resid_blocks = Z * Y * npd
    label_blocks = C // BLK
    t = lax.axis_index("tile")
    k = lax.axis_index("tok")
    z, y = t // Y, t % Y
    oy = Y - 1 - y
    has_r, has_l = z < Z - 1, z > 0
    mine = pl.ds(pl.multiple_of(k * CHUNK, CHUNK), CHUNK)
    other = pl.ds(pl.multiple_of((1 - k) * CHUNK, CHUNK), CHUNK)
    right, left, peer = {"tile": t + Y}, {"tile": t - Y}, {"tile": z * Y + oy}
    sib = {"tok": 1 - k}

    def two_way(c):
        return Y > 1 and c > 0

    def cell(c, zz, yy):
        return g[c].at[pl.ds((yy * Z + zz) * npd, npd), mine, :]

    def remote(way, c, zz, yy):
        part = cell(c, zz, yy)
        return pltpu.make_async_remote_copy(
            src_ref=part,
            dst_ref=part,
            send_sem=ssem.at[way, c, yy * Z + zz],
            recv_sem=rsem.at[c, yy * Z + zz],
            device_id=(right, left, peer)[way],
            device_id_type=MESH,
        )

    def across(c, yy, half):
        part = g[c].at[pl.ds(yy * Z * npd, Z * npd), half, :]
        return pltpu.make_async_remote_copy(
            src_ref=part,
            dst_ref=part,
            send_sem=xs.at[c, yy],
            recv_sem=xr.at[c, yy],
            device_id=sib,
            device_id_type=MESH,
        )

    for c in range(n):
        for j in range(npd):
            pltpu.make_async_copy(
                x_ref.at[pl.ds(c * CHUNK, CHUNK), pl.ds(j * BLK, BLK)],
                g[c].at[(y * Z + z) * npd + j, mine, :],
                lsem.at[c],
            ).start()

    barrier = pltpu.get_barrier_semaphore()

    @pl.when(has_r)
    def _():
        pl.semaphore_signal(barrier, inc=1, device_id=right, device_id_type=MESH)

    @pl.when(has_l)
    def _():
        pl.semaphore_signal(barrier, inc=1, device_id=left, device_id_type=MESH)

    if Y > 1:
        pl.semaphore_signal(barrier, inc=1, device_id=peer, device_id_type=MESH)
    pl.semaphore_signal(barrier, inc=1, device_id=sib, device_id_type=MESH)
    near = 1 + (Y > 1)
    pl.semaphore_wait(barrier, near + jnp.where(has_r, 1, 0) + jnp.where(has_l, 1, 0))

    def push(c, zz, yy):
        @pl.when(has_r)
        def _():
            remote(0, c, zz, yy).start()

        @pl.when(has_l)
        def _():
            remote(1, c, zz, yy).start()

    def own_here(c):
        pltpu.make_async_copy(cell(c, z, y), cell(c, z, y), lsem.at[c]).wait()

    def along(c, j, yy):
        @pl.when(z - j >= 0)
        def _():
            remote(0, c, z - j, yy).wait_recv()

            @pl.when(has_r)
            def _():
                remote(0, c, z - j, yy).start()

            if two_way(c):
                remote(2, c, z - j, yy).start()

        @pl.when(z + j < Z)
        def _():
            remote(1, c, z + j, yy).wait_recv()

            @pl.when(has_l)
            def _():
                remote(1, c, z + j, yy).start()

            if two_way(c):
                remote(2, c, z + j, yy).start()

    def from_peer(c, j):
        @pl.when(z - j >= 0)
        def _():
            remote(2, c, z - j, oy).wait_recv()

        @pl.when(z + j < Z)
        def _():
            remote(2, c, z + j, oy).wait_recv()

    def wait_sent(c):
        rows = [y] if two_way(c) or Y == 1 else [y, oy]

        def one(zz, _):
            for yy in rows:
                @pl.when(has_r & (zz <= z))
                def _():
                    remote(0, c, zz, yy).wait_send()

                @pl.when(has_l & (zz >= z))
                def _():
                    remote(1, c, zz, yy).wait_send()

            if two_way(c):
                remote(2, c, zz, y).wait_send()
            return 0

        lax.fori_loop(0, Z, one, 0)
        if Y > 1 and not two_way(c):
            remote(2, c, z, y).wait_send()
        for yy in range(Y):
            across(c, yy, mine).wait_send()

    def label_rows(c):
        marks = lab_ref[c]
        lanes = lax.broadcasted_iota(jnp.int32, (2 * CHUNK, BLK), 1)
        for h in range(label_blocks):
            hit = marks == lanes + h * BLK
            g[c][resid_blocks + h] = jnp.where(hit, 1.0, 0.0).astype(jnp.bfloat16)

    def column_sums(c):
        def one(b, _):
            part = jnp.sum(g[c][b].astype(jnp.float32), 0, keepdims=True)
            sums[b] = part if c == 0 else sums[b] + part
            return 0

        lax.fori_loop(0, resid_blocks + label_blocks, one, 0)

    def product(c, i):
        lhs = g[c][idx_ref[i, 0]]
        parts = []
        for h in range(TILE // BLK):
            rhs = g[c][idx_ref[i, 1 + h]]
            parts.append(
                lax.dot_general(
                    lhs, rhs, (((0,), (0,)), ((), ())), preferred_element_type=jnp.float32
                )
            )
        return parts

    def add_tiles(c, lo, hi):
        def one(i, _):
            for h, part in enumerate(product(c, i)):
                cols = slice(h * BLK, (h + 1) * BLK)
                acc[i, :, cols] = part if c == 0 else acc[i, :, cols] + part
            return 0

        lax.fori_loop(lo, hi, one, 0)

    def finish(c):
        def one(i, _):
            keep = idx_ref[i, 3] > 0
            row = jnp.broadcast_to(sums[idx_ref[i, 0]] / total_rows, (8, BLK))
            col = jnp.transpose(row)[:, :1]
            for h, part in enumerate(product(c, i)):
                cols = slice(h * BLK, (h + 1) * BLK)
                mean = sums[idx_ref[i, 1 + h]] / total_rows
                value = (acc[i, :, cols] + part) / total_rows - col * mean
                acc[i, :, cols] = jnp.where(keep, value, 0.0)
            pltpu.make_async_copy(acc.at[i], out_ref.at[i], osem).start()
            return 0

        lax.fori_loop(0, own, one, 0)

    own_here(0)
    push(0, z, y)
    if Y > 1:
        remote(2, 0, z, y).start()
    for c in range(1, n):
        own_here(c)
        if c == 1:
            push(1, z, y)
        if Y > 1:
            remote(2, c, z, y).start()

    for ph in range(n + 1):
        if ph > 0 and ph + 1 < n:
            push(ph + 1, z, y)
        if ph < n:
            label_rows(ph)
            if Y > 1 and not two_way(ph):
                remote(2, ph, z, oy).wait_recv()
                push(ph, z, oy)
        done = ph - 2
        if done >= 0:
            for yy in range(Y):
                across(done, yy, other).wait_recv()
            column_sums(done)
        if 1 <= ph and two_way(ph - 1):
            remote(2, ph - 1, z, oy).wait_recv()

        def step(j, _):
            if ph < n:
                along(ph, j, y)
                if Y > 1 and not two_way(ph):
                    along(ph, j, oy)
            if ph >= 1 and two_way(ph - 1):
                from_peer(ph - 1, j)
            if done >= 0:
                add_tiles(done, (j - 1) * own // (Z - 1), j * own // (Z - 1))
            return 0

        lax.fori_loop(1, Z, step, 0)
        if ph < n:
            across(ph, y, mine).start()
            if Y > 1 and not two_way(ph):
                across(ph, oy, mine).start()
        if ph >= 1 and two_way(ph - 1):
            across(ph - 1, oy, mine).start()
        if done >= 0:
            wait_sent(done)

    for yy in range(Y):
        across(n - 1, yy, other).wait_recv()
    column_sums(n - 1)
    finish(n - 1)
    wait_sent(n - 1)
    pltpu.make_async_copy(acc, out_ref, osem).wait()


def body(cfg, resid, labels, owner):
    n, Z, Y, npd, own, total_rows = cfg
    place = lax.axis_index("tile")
    half = lax.axis_index("tok")
    inverse = (
        jnp.full(owner.shape, TASKS, jnp.int32)
        .at[owner[:TASKS]]
        .set(jnp.arange(TASKS, dtype=jnp.int32))
    )
    tasks = lax.dynamic_slice_in_dim(inverse, place * own, own)

    resid_blocks = Z * Y * npd
    spot = np.arange(PANELS * TILE // BLK)
    source = spot // npd
    held = ((source % Y) * Z + source // Y) * npd + spot % npd
    spot = np.where(spot < resid_blocks, held, spot).astype(np.int32)
    pairs = pair_table(PANELS)
    firsts, seconds = pairs[:, 0], pairs[:, 1]
    table = np.stack(
        [spot[2 * firsts], spot[2 * firsts + 1], spot[2 * seconds], spot[2 * seconds + 1],
         np.ones(TASKS, np.int32)], 1)
    table = jnp.asarray(np.concatenate([table, np.zeros((1, 5), np.int32)], 0))
    rows = table[tasks]
    lead = jnp.where(half == 0, rows[:, 0], rows[:, 1])
    idx = jnp.stack([lead, rows[:, 2], rows[:, 3], rows[:, 4]], 1)
    marks = labels.reshape(2, n, CHUNK).transpose(1, 0, 2).reshape(n, 2 * CHUNK, 1)

    blocks = PANELS * TILE // BLK
    flops = 2 * own * TILE // 2 * TILE * total_rows
    return pl.pallas_call(
        functools.partial(kernel, cfg),
        out_shape=jax.ShapeDtypeStruct((own, BLK, TILE), jnp.float32),
        in_specs=[
            pl.BlockSpec(memory_space=pltpu.SMEM),
            pl.BlockSpec(memory_space=pltpu.VMEM),
            pl.BlockSpec(memory_space=pl.ANY),
        ],
        out_specs=pl.BlockSpec(memory_space=pl.ANY),
        scratch_shapes=[pltpu.VMEM((blocks, 2 * CHUNK, BLK), jnp.bfloat16) for _ in range(n)]
        + [
            pltpu.VMEM((own, BLK, TILE), jnp.float32),
            pltpu.VMEM((blocks, 1, BLK), jnp.float32),
            pltpu.SemaphoreType.DMA((n,)),
            pltpu.SemaphoreType.DMA,
            pltpu.SemaphoreType.DMA((n, Z * Y)),
            pltpu.SemaphoreType.DMA((3, n, Z * Y)),
            pltpu.SemaphoreType.DMA((n, Y)),
            pltpu.SemaphoreType.DMA((n, Y)),
        ],
        compiler_params=pltpu.CompilerParams(
            collective_id=0, has_side_effects=True, vmem_limit_bytes=60 * 1024 * 1024
        ),
        cost_estimate=pl.CostEstimate(
            flops=flops, bytes_accessed=own * BLK * TILE * 4, transcendentals=0
        ),
    )(idx, marks, resid)


def solution(mesh):
    tiles = mesh.shape["tile"]

    def whole(resid, labels, owner):
        here = resid.shape[0] // mesh.shape["grp"] // mesh.shape["tok"]
        Y = 2 if tiles <= 8 else 1
        cfg = (
            here // CHUNK,
            tiles // Y,
            Y,
            resid.shape[1] // tiles // BLK,
            owner.shape[0] // tiles,
            labels.shape[0] // mesh.shape["grp"],
        )
        return jax.shard_map(
            functools.partial(body, cfg),
            mesh=mesh,
            in_specs=(P(("grp", "tok"), "tile"), P("grp"), P()),
            out_specs=P(("grp", "tile"), "tok", None),
            check_vma=False,
        )(resid, labels, owner)

    return whole
```

time: 536 us -> 194 us (0.36)
  waiting for transfers between devices: 202 us -> 0 us
  Pallas kernels: 0 us -> 174 us
  local copies, waits for them, and re-layouts: 111 us -> 17.9 us
  matrix products: 86.4 us -> 0 us
  loops' own time: 71.6 us -> 0 us
  other arithmetic: 44.7 us -> 1.52 us
  between operations: 13.5 us -> 0.02 us
    all_gather x1 -> x0, waiting for transfers between devices: 202 us -> none  [body(): columns = lax.all_gather(resid, 'tile', axis=1, tiled=True)]
    pallas_call x0 -> x1, Pallas kernels: none -> 174 us  [body(): pl.pallas_call(functools.partial(kernel, cfg), out_shape=jax.ShapeDtypeSt...]
    dot_general x27 -> x0, matrix products: 86.4 us -> none  [dense_rows(): lax.dot_general(left, right, (((0,), (0,)), ((), ())), preferred_element_...]
    gather x164 -> x1, local copies, waits for them, and re-layouts: 73.8 us -> 1.46 us  [body(): rows = table[tasks]]
    another operation x3 -> x0, loops' own time: 71.6 us -> none  [the longest x1 70.6 us: owned_tiles(): return lax.map(owned_one, tasks)]
    dynamic_slice x55 -> x0, local copies, waits for them, and re-layouts: 36 us -> none  [the longest x27 17.6 us: owned_one(): first = pairs[pick, 0]]
    concatenate x2 -> x0, other arithmetic: 18.9 us -> none  [the longest x1 18.9 us: body(): matrix = jnp.concatenate([columns, label_panel(marks)], 1)]
    unnamed x2 -> x1, local copies, waits for them, and re-layouts: 0.01 us -> 13.2 us
  transfers between devices with their start and end apart: 2 -> 0, of which waited for: 1 -> 0; matrix products, arithmetic and copies ran while one was open for 17% -> 0% of each run, Pallas kernels for 0% -> 0%
where the time goes in v1:
time: 194 us; the launch traced here: 193 us
  Pallas kernels  174 us (90%)
  local copies, waits for them, and re-layouts  17.9 us (9%)
    pallas_call x1, Pallas kernels, body(): pl.pallas_call(functools.partial(kernel, cfg), out_shape=jax.ShapeDtypeSt...  174 us
    unnamed x1, local copies, waits for them, and re-layouts  13.2 us

profile of v1, /device:TPU:0, one launch (start us, length us, event | category | flops | bytes accessed | tf_op | source)
XLA Modules:
  0.0 193.5 jit_solution(1294300636144557746)
XLA Ops:
  0.0 0.7 compare_select_fusion
  0.7 1.2 scatter_custom_fusion
  1.9 0.1 compare_select_fusion.1
  2.0 0.7 reshape.6
  2.7 1.5 gather_fusion
  4.2 0.1 slice_select_fusion
  4.3 0.1 slice.23
  4.3 0.7 pad_add_fusion.idx_ref
  5.0 1.3 copy.10.lab_ref
  6.3 174.0 %shard_map.46 = f32[27,256,512]{2,1,0:T(8,128)} custom-call(s32[27,4]{1,0:T(8,128)} %pad_add_fusion.idx_ref, s32[7,256,1]{2,1,0:T(8,128)} %copy.10.lab_ref, bf16[896,1024]{1,0:T(8,128)(2,1)} %x_ref.1), custom_call_target="tpu_custom_call" | custom-call | flops 12683575296 | bytes 14155776 | tf_op jit(solution)/shard_map/pallas_call | solution.py:296
  180.3 13.2 %copy.12 = f32[27,256,512]{2,1,0:T(8,128)} copy(f32[27,256,512]{2,1,0:T(8,128)} %shard_map.46) | data formatting | bytes 28311552
  (2 shorter events, 0.0 us)

commit v2 on v1

--- a/solution.py
+++ b/solution.py
@@ -22,10 +22,40 @@
     return np.stack([firsts, seconds], 1).astype(np.int32)
 
 
-def kernel(cfg, idx_ref, lab_ref, x_ref, out_ref, *scratch):
+def products(blocks, idx_ref, i):
+    lhs = blocks[idx_ref[i, 0]]
+    parts = []
+    for h in range(TILE // BLK):
+        rhs = blocks[idx_ref[i, 1 + h]]
+        parts.append(
+            lax.dot_general(
+                lhs, rhs, (((0,), (0,)), ((), ())), preferred_element_type=jnp.float32
+            )
+        )
+    return parts
+
+
+def finish(total_rows, idx_ref, sums, acc, out_ref, tiles, sem):
+    scale = 1.0 / total_rows
+
+    def one(i, _):
+        keep = jnp.where(idx_ref[i, 3] > 0, scale, 0.0)
+        row = jnp.broadcast_to(sums[idx_ref[i, 0]] * scale, (8, BLK))
+        col = jnp.transpose(row)[:, :1]
+        for h in range(TILE // BLK):
+            cols = slice(h * BLK, (h + 1) * BLK)
+            tiles[i, :, cols] = (acc[i, :, cols] - col * sums[idx_ref[i, 1 + h]]) * keep
+        pltpu.make_async_copy(tiles.at[i], out_ref.at[i], sem).start()
+        return 0
+
+    lax.fori_loop(0, tiles.shape[0], one, 0)
+    pltpu.make_async_copy(tiles, out_ref, sem).wait()
+
+
+def kernel(cfg, idx_ref, lab_ref, x_ref, acc, sums, *scratch):
     n, Z, Y, npd, own, total_rows = cfg
     g = scratch[:n]
-    acc, sums, lsem, osem, rsem, ssem, xs, xr = scratch[n:]
+    lsem, rsem, ssem, xs, xr = scratch[n:]
     resid_blocks = Z * Y * npd
     label_blocks = C // BLK
     t = lax.axis_index("tile")
@@ -164,49 +194,22 @@
             hit = marks == lanes + h * BLK
             g[c][resid_blocks + h] = jnp.where(hit, 1.0, 0.0).astype(jnp.bfloat16)
 
-    def column_sums(c):
+    def column_sums(c, first, count):
         def one(b, _):
             part = jnp.sum(g[c][b].astype(jnp.float32), 0, keepdims=True)
             sums[b] = part if c == 0 else sums[b] + part
             return 0
 
-        lax.fori_loop(0, resid_blocks + label_blocks, one, 0)
-
-    def product(c, i):
-        lhs = g[c][idx_ref[i, 0]]
-        parts = []
-        for h in range(TILE // BLK):
-            rhs = g[c][idx_ref[i, 1 + h]]
-            parts.append(
-                lax.dot_general(
-                    lhs, rhs, (((0,), (0,)), ((), ())), preferred_element_type=jnp.float32
-                )
-            )
-        return parts
+        lax.fori_loop(first, first + count, one, 0)
 
     def add_tiles(c, lo, hi):
         def one(i, _):
-            for h, part in enumerate(product(c, i)):
+            for h, part in enumerate(products(g[c], idx_ref, i)):
                 cols = slice(h * BLK, (h + 1) * BLK)
                 acc[i, :, cols] = part if c == 0 else acc[i, :, cols] + part
             return 0
 
         lax.fori_loop(lo, hi, one, 0)
-
-    def finish(c):
-        def one(i, _):
-            keep = idx_ref[i, 3] > 0
-            row = jnp.broadcast_to(sums[idx_ref[i, 0]] / total_rows, (8, BLK))
-            col = jnp.transpose(row)[:, :1]
-            for h, part in enumerate(product(c, i)):
-                cols = slice(h * BLK, (h + 1) * BLK)
-                mean = sums[idx_ref[i, 1 + h]] / total_rows
-                value = (acc[i, :, cols] + part) / total_rows - col * mean
-                acc[i, :, cols] = jnp.where(keep, value, 0.0)
-            pltpu.make_async_copy(acc.at[i], out_ref.at[i], osem).start()
-            return 0
-
-        lax.fori_loop(0, own, one, 0)
 
     own_here(0)
     push(0, z, y)
@@ -231,7 +234,7 @@
         if done >= 0:
             for yy in range(Y):
                 across(done, yy, other).wait_recv()
-            column_sums(done)
+            column_sums(done, 0, resid_blocks + label_blocks)
         if 1 <= ph and two_way(ph - 1):
             remote(2, ph - 1, z, oy).wait_recv()
 
@@ -256,12 +259,15 @@
         if done >= 0:
             wait_sent(done)
 
-    for yy in range(Y):
-        across(n - 1, yy, other).wait_recv()
-    column_sums(n - 1)
-    finish(n - 1)
+    row_blocks = Z * npd
+    across(n - 1, y, other).wait_recv()
+    column_sums(n - 1, y * row_blocks, row_blocks)
+    column_sums(n - 1, resid_blocks, label_blocks)
+    if Y > 1:
+        across(n - 1, oy, other).wait_recv()
+        column_sums(n - 1, oy * row_blocks, row_blocks)
+    add_tiles(n - 1, 0, own)
     wait_sent(n - 1)
-    pltpu.make_async_copy(acc, out_ref, osem).wait()
 
 
 def body(cfg, resid, labels, owner):
@@ -293,33 +299,52 @@
 
     blocks = PANELS * TILE // BLK
     flops = 2 * own * TILE // 2 * TILE * total_rows
-    return pl.pallas_call(
+    acc, sums = pl.pallas_call(
         functools.partial(kernel, cfg),
-        out_shape=jax.ShapeDtypeStruct((own, BLK, TILE), jnp.float32),
+        out_shape=[
+            pltpu.VMEM((own, BLK, TILE), jnp.float32),
+            pltpu.VMEM((blocks, 1, BLK), jnp.float32),
+        ],
         in_specs=[
             pl.BlockSpec(memory_space=pltpu.SMEM),
             pl.BlockSpec(memory_space=pltpu.VMEM),
             pl.BlockSpec(memory_space=pl.ANY),
         ],
-        out_specs=pl.BlockSpec(memory_space=pl.ANY),
+        out_specs=[pl.BlockSpec(memory_space=pltpu.VMEM)] * 2,
         scratch_shapes=[pltpu.VMEM((blocks, 2 * CHUNK, BLK), jnp.bfloat16) for _ in range(n)]
         + [
-            pltpu.VMEM((own, BLK, TILE), jnp.float32),
-            pltpu.VMEM((blocks, 1, BLK), jnp.float32),
             pltpu.SemaphoreType.DMA((n,)),
-            pltpu.SemaphoreType.DMA,
             pltpu.SemaphoreType.DMA((n, Z * Y)),
             pltpu.SemaphoreType.DMA((3, n, Z * Y)),
             pltpu.SemaphoreType.DMA((n, Y)),
             pltpu.SemaphoreType.DMA((n, Y)),
         ],
         compiler_params=pltpu.CompilerParams(
-            collective_id=0, has_side_effects=True, vmem_limit_bytes=60 * 1024 * 1024
+            collective_id=0, has_side_effects=True, vmem_limit_bytes=38 * 1024 * 1024
         ),
         cost_estimate=pl.CostEstimate(
             flops=flops, bytes_accessed=own * BLK * TILE * 4, transcendentals=0
         ),
     )(idx, marks, resid)
+    acc, sums = (pltpu.with_memory_space_constraint(a, pltpu.VMEM) for a in (acc, sums))
+    return pl.pallas_call(
+        functools.partial(finish, total_rows),
+        out_shape=jax.ShapeDtypeStruct((own, BLK, TILE), jnp.float32),
+        in_specs=[
+            pl.BlockSpec(memory_space=pltpu.SMEM),
+            pl.BlockSpec(memory_space=pltpu.VMEM),
+            pl.BlockSpec(memory_space=pltpu.VMEM),
+        ],
+        out_specs=pl.BlockSpec(memory_space=pl.ANY),
+        scratch_shapes=[
+            pltpu.VMEM((own, BLK, TILE), jnp.float32),
+            pltpu.SemaphoreType.DMA,
+        ],
+        compiler_params=pltpu.CompilerParams(vmem_limit_bytes=20 * 1024 * 1024),
+        cost_estimate=pl.CostEstimate(
+            flops=3 * own * BLK * TILE, bytes_accessed=own * BLK * TILE * 4, transcendentals=0
+        ),
+    )(idx, sums, acc)
 
 
 def solution(mesh):

time: 194 us -> 184 us (0.948)
  local copies, waits for them, and re-layouts: 17.9 us -> 3.82 us
  Pallas kernels: 174 us -> 179 us
    unnamed x1 -> x0, local copies, waits for them, and re-layouts: 13.2 us -> none
    pallas_call x1 -> x2, Pallas kernels: 174 us -> 179 us  [the longest x1 170 us: body(): pl.pallas_call(functools.partial(kernel, cfg), out_shape=[pltpu.VMEM((own...]
where the time goes in v2:
time: 184 us
  Pallas kernels  179 us (97%)
  local copies, waits for them, and re-layouts  3.82 us (2%)
    pallas_call x1, Pallas kernels, body(): pl.pallas_call(functools.partial(kernel, cfg), out_shape=[pltpu.VMEM((own...  170 us
    pallas_call x1, Pallas kernels, body(): pl.pallas_call(functools.partial(finish, total_rows), out_shape=jax.Shape...  8.63 us

profile of v2, /device:TPU:0, one launch (start us, length us, event | category | flops | bytes accessed | tf_op | source)
XLA Modules:
  0.0 183.7 jit_solution(13952958700345698412)
XLA Ops:
  0.0 0.7 compare_select_fusion
  0.7 1.2 scatter_custom_fusion
  1.9 0.1 compare_select_fusion.1
  2.0 0.7 reshape.6
  2.7 1.5 gather_fusion
  4.2 0.1 slice_select_fusion
  4.3 0.1 slice.23
  4.3 0.1 pad_add_fusion.idx_ref
  4.4 0.3 copy.11.lab_ref
  4.8 170.3 %shard_map.46 = (f32[27,256,512]{2,1,0:T(8,128)S(1)}, f32[40,1,256]{2,1,0:T(1,128)S(1)}) custom-call(s32[27,4]{1,0:T(8,128)S(1)} %pad_add_fusion.idx_ref, s32[7,256,1]{2,1,0:T(8,128)S(1)} %copy.11.lab_ref, bf16[896,1024]{1,0:T(8,128)(2,1)} %x_ref.1), custom_call_target="tpu_custom_call" | custom-call | flops 12683575296 | bytes 14155776 | tf_op jit(solution)/shard_map/pallas_call | solution.py:302
  175.1 8.6 %shard_map.47 = f32[27,256,512]{2,1,0:T(8,128)} custom-call(s32[27,4]{1,0:T(8,128)S(1)} %pad_add_fusion.idx_ref, f32[40,1,256]{2,1,0:T(1,128)S(1)} %get-tuple-element.7.sums, f32[27,256,512]{2,1,0:T(8,128)S(1)} %get-tuple-element.8.acc), custom_call_target="tpu_custom_call" | custom-call | flops 10616832 | bytes 14155776 | tf_op jit(solution)/shard_map/pallas_call | solution.py:330
  (2 shorter events, 0.0 us)

commit v3 on v2

--- a/solution.py
+++ b/solution.py
@@ -35,16 +35,17 @@
     return parts
 
 
-def finish(total_rows, idx_ref, sums, acc, out_ref, tiles, sem):
+def finish(total_rows, idx_ref, sums, acc, last, out_ref, tiles, sem):
     scale = 1.0 / total_rows
 
     def one(i, _):
         keep = jnp.where(idx_ref[i, 3] > 0, scale, 0.0)
         row = jnp.broadcast_to(sums[idx_ref[i, 0]] * scale, (8, BLK))
         col = jnp.transpose(row)[:, :1]
-        for h in range(TILE // BLK):
+        for h, part in enumerate(products(last, idx_ref, i)):
             cols = slice(h * BLK, (h + 1) * BLK)
-            tiles[i, :, cols] = (acc[i, :, cols] - col * sums[idx_ref[i, 1 + h]]) * keep
+            gram = acc[i, :, cols] + part
+            tiles[i, :, cols] = (gram - col * sums[idx_ref[i, 1 + h]]) * keep
         pltpu.make_async_copy(tiles.at[i], out_ref.at[i], sem).start()
         return 0
 
@@ -52,10 +53,10 @@
     pltpu.make_async_copy(tiles, out_ref, sem).wait()
 
 
-def kernel(cfg, idx_ref, lab_ref, x_ref, acc, sums, *scratch):
+def kernel(cfg, idx_ref, lab_ref, x_ref, acc, sums, last, *scratch):
     n, Z, Y, npd, own, total_rows = cfg
-    g = scratch[:n]
-    lsem, rsem, ssem, xs, xr = scratch[n:]
+    g = scratch[: n - 1] + (last,)
+    lsem, rsem, ssem, xs, xr = scratch[n - 1 :]
     resid_blocks = Z * Y * npd
     label_blocks = C // BLK
     t = lax.axis_index("tile")
@@ -235,6 +236,11 @@
             for yy in range(Y):
                 across(done, yy, other).wait_recv()
             column_sums(done, 0, resid_blocks + label_blocks)
+        if ph == n:
+            across(n - 1, y, other).wait_recv()
+            column_sums(n - 1, y * Z * npd, Z * npd)
+            column_sums(n - 1, resid_blocks, label_blocks)
+            add_tiles(done, 0, own)
         if 1 <= ph and two_way(ph - 1):
             remote(2, ph - 1, z, oy).wait_recv()
 
@@ -245,7 +251,7 @@
                     along(ph, j, oy)
             if ph >= 1 and two_way(ph - 1):
                 from_peer(ph - 1, j)
-            if done >= 0:
+            if 0 <= done and ph < n:
                 add_tiles(done, (j - 1) * own // (Z - 1), j * own // (Z - 1))
             return 0
 
@@ -259,14 +265,9 @@
         if done >= 0:
             wait_sent(done)
 
-    row_blocks = Z * npd
-    across(n - 1, y, other).wait_recv()
-    column_sums(n - 1, y * row_blocks, row_blocks)
-    column_sums(n - 1, resid_blocks, label_blocks)
     if Y > 1:
         across(n - 1, oy, other).wait_recv()
-        column_sums(n - 1, oy * row_blocks, row_blocks)
-    add_tiles(n - 1, 0, own)
+        column_sums(n - 1, oy * Z * npd, Z * npd)
     wait_sent(n - 1)
 
 
@@ -274,13 +275,6 @@
     n, Z, Y, npd, own, total_rows = cfg
     place = lax.axis_index("tile")
     half = lax.axis_index("tok")
-    inverse = (
-        jnp.full(owner.shape, TASKS, jnp.int32)
-        .at[owner[:TASKS]]
-        .set(jnp.arange(TASKS, dtype=jnp.int32))
-    )
-    tasks = lax.dynamic_slice_in_dim(inverse, place * own, own)
-
     resid_blocks = Z * Y * npd
     spot = np.arange(PANELS * TILE // BLK)
     source = spot // npd
@@ -288,30 +282,30 @@
     spot = np.where(spot < resid_blocks, held, spot).astype(np.int32)
     pairs = pair_table(PANELS)
     firsts, seconds = pairs[:, 0], pairs[:, 1]
-    table = np.stack(
-        [spot[2 * firsts], spot[2 * firsts + 1], spot[2 * seconds], spot[2 * seconds + 1],
-         np.ones(TASKS, np.int32)], 1)
-    table = jnp.asarray(np.concatenate([table, np.zeros((1, 5), np.int32)], 0))
-    rows = table[tasks]
-    lead = jnp.where(half == 0, rows[:, 0], rows[:, 1])
-    idx = jnp.stack([lead, rows[:, 2], rows[:, 3], rows[:, 4]], 1)
+    leads = jnp.where(half == 0, spot[2 * firsts], spot[2 * firsts + 1])
+    columns = [leads, spot[2 * seconds], spot[2 * seconds + 1], np.ones(TASKS, np.int32)]
+    table = jnp.stack([jnp.asarray(column) for column in columns])
+    slots = place * own + jnp.arange(own, dtype=jnp.int32)
+    found = owner[None, None, :TASKS] == slots[:, None, None]
+    idx = jnp.sum(jnp.where(found, table[None], 0), 2)
     marks = labels.reshape(2, n, CHUNK).transpose(1, 0, 2).reshape(n, 2 * CHUNK, 1)
 
     blocks = PANELS * TILE // BLK
     flops = 2 * own * TILE // 2 * TILE * total_rows
-    acc, sums = pl.pallas_call(
+    acc, sums, last = pl.pallas_call(
         functools.partial(kernel, cfg),
         out_shape=[
             pltpu.VMEM((own, BLK, TILE), jnp.float32),
             pltpu.VMEM((blocks, 1, BLK), jnp.float32),
+            pltpu.VMEM((blocks, 2 * CHUNK, BLK), jnp.bfloat16),
         ],
         in_specs=[
             pl.BlockSpec(memory_space=pltpu.SMEM),
             pl.BlockSpec(memory_space=pltpu.VMEM),
             pl.BlockSpec(memory_space=pl.ANY),
         ],
-        out_specs=[pl.BlockSpec(memory_space=pltpu.VMEM)] * 2,
-        scratch_shapes=[pltpu.VMEM((blocks, 2 * CHUNK, BLK), jnp.bfloat16) for _ in range(n)]
+        out_specs=[pl.BlockSpec(memory_space=pltpu.VMEM)] * 3,
+        scratch_shapes=[pltpu.VMEM((blocks, 2 * CHUNK, BLK), jnp.bfloat16) for _ in range(n - 1)]
         + [
             pltpu.SemaphoreType.DMA((n,)),
             pltpu.SemaphoreType.DMA((n, Z * Y)),
@@ -320,13 +314,13 @@
             pltpu.SemaphoreType.DMA((n, Y)),
         ],
         compiler_params=pltpu.CompilerParams(
-            collective_id=0, has_side_effects=True, vmem_limit_bytes=38 * 1024 * 1024
+            collective_id=0, has_side_effects=True, vmem_limit_bytes=32 * 1024 * 1024
         ),
         cost_estimate=pl.CostEstimate(
             flops=flops, bytes_accessed=own * BLK * TILE * 4, transcendentals=0
         ),
     )(idx, marks, resid)
-    acc, sums = (pltpu.with_memory_space_constraint(a, pltpu.VMEM) for a in (acc, sums))
+    held = [pltpu.with_memory_space_constraint(a, pltpu.VMEM) for a in (sums, acc, last)]
     return pl.pallas_call(
         functools.partial(finish, total_rows),
         out_shape=jax.ShapeDtypeStruct((own, BLK, TILE), jnp.float32),
@@ -334,17 +328,18 @@
             pl.BlockSpec(memory_space=pltpu.SMEM),
             pl.BlockSpec(memory_space=pltpu.VMEM),
             pl.BlockSpec(memory_space=pltpu.VMEM),
+            pl.BlockSpec(memory_space=pltpu.VMEM),
         ],
         out_specs=pl.BlockSpec(memory_space=pl.ANY),
         scratch_shapes=[
             pltpu.VMEM((own, BLK, TILE), jnp.float32),
             pltpu.SemaphoreType.DMA,
         ],
-        compiler_params=pltpu.CompilerParams(vmem_limit_bytes=20 * 1024 * 1024),
+        compiler_params=pltpu.CompilerParams(vmem_limit_bytes=14 * 1024 * 1024),
         cost_estimate=pl.CostEstimate(
-            flops=3 * own * BLK * TILE, bytes_accessed=own * BLK * TILE * 4, transcendentals=0
+            flops=flops // n, bytes_accessed=own * BLK * TILE * 4, transcendentals=0
         ),
-    )(idx, sums, acc)
+    )(idx, *held)
 
 
 def solution(mesh):

time: 184 us -> 179 us (0.973)
  Pallas kernels: 179 us -> 173 us
    pallas_call x1, Pallas kernels: 170 us -> 163 us  [body(): pl.pallas_call(functools.partial(kernel, cfg), out_shape=[pltpu.VMEM((own...]
where the time goes in v3:
time: 179 us; the launch traced here: 178 us
  Pallas kernels  173 us (97%)
  other arithmetic  2.76 us (2%)
  local copies, waits for them, and re-layouts  2.6 us (1%)
    pallas_call x1, Pallas kernels, body(): pl.pallas_call(functools.partial(kernel, cfg), out_shape=[pltpu.VMEM((own...  163 us
    pallas_call x1, Pallas kernels, body(): pl.pallas_call(functools.partial(finish, total_rows), out_shape=jax.Shape...  9.57 us

profile of v3, /device:TPU:0, one launch (start us, length us, event | category | flops | bytes accessed | tf_op | source)
XLA Modules:
  0.0 178.2 jit_solution(7091739603600629150)
XLA Ops:
  0.0 0.7 broadcast_select_fusion
  0.7 0.1 pad.3.clone
  0.8 0.8 add_add_fusion
  1.5 0.8 broadcast_compare_fusion
  2.3 0.6 select_reduce_fusion.idx_ref
  2.8 0.7 reshape.40
  3.5 0.3 copy.10.lab_ref
  3.9 0.0 copy-start
  3.9 1.5 copy-done
  5.4 163.3 %shard_map.82 = (f32[27,256,512]{2,1,0:T(8,128)S(1)}, f32[40,1,256]{2,1,0:T(1,128)S(1)}, bf16[40,256,256]{2,1,0:T(8,128)(2,1)S(1)}) custom-call(s32[27,4]{1,0:T(8,128)S(1)} %select_reduce_fusion.idx_ref, s32[7,256,1]{2,1,0:T(8,128)S(1)} %copy.10.lab_ref, bf16[896,1024]{1,0:T(8,128)(2,1)S(1)} %copy-done), custom_call_target="tpu_custom_call" | custom-call | flops 12683575296 | bytes 14155776 | tf_op jit(solution)/shard_map/pallas_call | solution.py:295
  168.7 9.6 %shard_map.83 = f32[27,256,512]{2,1,0:T(8,128)} custom-call(s32[27,4]{1,0:T(8,128)S(1)} %select_reduce_fusion.idx_ref, f32[40,1,256]{2,1,0:T(1,128)S(1)} %get-tuple-element.8.sums, f32[27,256,512]{2,1,0:T(8,128)S(1)} %get-tuple-element.9.acc, bf16[40,256,256]{2,1,0:T(8,128)(2,1)S(1)} %get-tuple-element.10.last), custom_call_target="tpu_custom_call" | custom-call | flops 1811939328 | bytes 14155776 | tf_op jit(solution)/shard_map/pallas_call | solution.py:324
  (1 shorter events, 0.0 us)
Async XLA Ops:
  3.9 1.5 copy-start

commit v4 on v3

--- a/solution.py
+++ b/solution.py
@@ -235,7 +235,8 @@
         if done >= 0:
             for yy in range(Y):
                 across(done, yy, other).wait_recv()
-            column_sums(done, 0, resid_blocks + label_blocks)
+            if ph == n:
+                column_sums(done, 0, resid_blocks + label_blocks)
         if ph == n:
             across(n - 1, y, other).wait_recv()
             column_sums(n - 1, y * Z * npd, Z * npd)
@@ -252,6 +253,9 @@
             if ph >= 1 and two_way(ph - 1):
                 from_peer(ph - 1, j)
             if 0 <= done and ph < n:
+                total = resid_blocks + label_blocks
+                begin = (j - 1) * total // (Z - 1)
+                column_sums(done, begin, j * total // (Z - 1) - begin)
                 add_tiles(done, (j - 1) * own // (Z - 1), j * own // (Z - 1))
             return 0
 
@@ -292,6 +296,7 @@
 
     blocks = PANELS * TILE // BLK
     flops = 2 * own * TILE // 2 * TILE * total_rows
+    resid = pltpu.with_memory_space_constraint(resid, pltpu.HBM)
     acc, sums, last = pl.pallas_call(
         functools.partial(kernel, cfg),
         out_shape=[

time: 179 us -> 178 us (level)
  no operation moved by 1% of the time
where the time goes in v4:
time: 178 us
  Pallas kernels  174 us (98%)
  other arithmetic  2.76 us (2%)
    pallas_call x1, Pallas kernels, body(): pl.pallas_call(functools.partial(kernel, cfg), out_shape=[pltpu.VMEM((own...  165 us
    pallas_call x1, Pallas kernels, body(): pl.pallas_call(functools.partial(finish, total_rows), out_shape=jax.Shape...  9.58 us

profile of v4, /device:TPU:0, one launch (start us, length us, event | category | flops | bytes accessed | tf_op | source)
XLA Modules:
  0.0 178.2 jit_solution(10860711857630975434)
XLA Ops:
  0.0 0.7 broadcast_select_fusion
  0.7 0.1 pad.3.clone
  0.8 0.8 add_add_fusion
  1.5 0.8 broadcast_compare_fusion
  2.3 0.6 select_reduce_fusion.idx_ref
  2.8 0.7 reshape.40
  3.5 0.3 copy.10.lab_ref
  3.9 164.7 %shard_map.82 = (f32[27,256,512]{2,1,0:T(8,128)S(1)}, f32[40,1,256]{2,1,0:T(1,128)S(1)}, bf16[40,256,256]{2,1,0:T(8,128)(2,1)S(1)}) custom-call(s32[27,4]{1,0:T(8,128)S(1)} %select_reduce_fusion.idx_ref, s32[7,256,1]{2,1,0:T(8,128)S(1)} %copy.10.lab_ref, bf16[896,1024]{1,0:T(8,128)(2,1)} %x_ref.1), custom_call_target="tpu_custom_call" | custom-call | flops 12683575296 | bytes 14155776 | tf_op jit(solution)/shard_map/pallas_call | solution.py:300
  168.6 9.6 %shard_map.83 = f32[27,256,512]{2,1,0:T(8,128)} custom-call(s32[27,4]{1,0:T(8,128)S(1)} %select_reduce_fusion.idx_ref, f32[40,1,256]{2,1,0:T(1,128)S(1)} %get-tuple-element.8.sums, f32[27,256,512]{2,1,0:T(8,128)S(1)} %get-tuple-element.9.acc, bf16[40,256,256]{2,1,0:T(8,128)(2,1)S(1)} %get-tuple-element.10.last), custom_call_target="tpu_custom_call" | custom-call | flops 1811939328 | bytes 14155776 | tf_op jit(solution)/shard_map/pallas_call | solution.py:329
  (1 shorter events, 0.0 us)
